TPU v7x, 128 devices: a whole 4x4x4 slice. The times are simulated.
128 devices in a mesh: grp: 16 (over z, y_lo, core), tp: 8 (over x, y_hi).
Axes of the slice: x: 4, y: 4 (y_hi: 2, y_lo: 2; y = y_hi * 2 + y_lo), z: 4, core: 2. Of those that a mesh axis runs over, the one named last changes fastest.
Arguments:
- hidden: bfloat16 [512, 16384], P(('grp', 'tp')), may hold values from -130 to 130
- gain: float32 [16384], replicated, may hold values from 0.5 to 1.5
- head: bfloat16 [16384, 65536], P(None, ('grp', 'tp')), may hold values from -3 to 3
Outputs:
- log_probs: float32 [512, 65536], P(('grp', 'tp'))
All inputs are finite; a program needn't handle non-finite values.
Results may differ from a plain program's by a relative error of at most 0.00055.
Values may be sent and summed in bfloat16 or wider, within the bound.
A program may use at most 128 MiB of HBM per device.

v0:
```python
import jax
import jax.numpy as jnp
from jax import lax
from jax.sharding import PartitionSpec as P


def in_order(pieces, dim):
    pieces = jnp.moveaxis(pieces, 0, dim)
    dims = pieces.shape
    return pieces.reshape(*dims[:dim], dims[dim] * dims[dim + 1], *dims[dim + 2 :])


def sent_to_all(array, axis):
    count = lax.axis_size(axis)
    return lax.all_to_all(
        jnp.broadcast_to(array[None], (count, *array.shape)), axis, 0, 0, tiled=True
    )


def collect(array, axis, dim):
    return in_order(sent_to_all(array, axis), dim)


def on_device(hidden, gain, head):
    values = hidden.astype(jnp.float32)
    mean_square = jnp.mean(values * values, axis=-1, keepdims=True)
    normed = (values * lax.rsqrt(mean_square + 1e-05) * gain).astype(jnp.bfloat16)
    group_block = collect(normed, "tp", 0)
    logits = jnp.dot(
        lax.all_gather(group_block, "grp", axis=0, tiled=True),
        head,
        preferred_element_type=jnp.float32,
    )
    owned = lax.all_to_all(logits, ("grp", "tp"), split_axis=0, concat_axis=1, tiled=True)
    top = jnp.max(owned, axis=-1, keepdims=True)
    total = jnp.sum(jnp.exp(owned - top), axis=-1, keepdims=True)
    return owned - top - jnp.log(total)


def solution(mesh):
    return jax.shard_map(
        on_device,
        mesh=mesh,
        in_specs=(P(("grp", "tp"), None), P(), P(None, ("grp", "tp"))),
        out_specs=P(("grp", "tp"), None),
        check_vma=False,
    )
```

profile of v0, /device:TPU:1, one launch (start us, length us, event | category | flops | bytes accessed | tf_op | source)
XLA Modules:
  0.0 179.9 jit_solution(17725672794546746063)
XLA Ops:
  6.5 0.0 all-gather.2.cloned.1.call-start
  6.5 1.2 fusion.2
  7.7 1.0 fusion.4
  8.7 0.3 broadcast_in_dim.2
  9.0 22.5 %all_to_all.24 = bf16[8,4,16384]{2,1,0:T(4,128)(2,1)S(1)} all-to-all(bf16[8,4,16384]{2,1,0:T(4,128)(2,1)S(1)} %broadcast_in_dim.2), channel_id=1, replica_groups=mesh['grp'=16,'tp'=8] {'tp'}, dimensions={0} | all-to-all | bytes 2097152 | tf_op jit(solution)/shard_map/all_to_all | solution.py:15
  31.6 1.1 reshape.25
  32.6 0.0 all-gather.2.cloned.1.call-update
  32.7 92.8 %all-gather.2.cloned.1.call-done = bf16[512,16384]{1,0:T(8,128)(2,1)} async-done(((bf16[32,16384]{1,0:T(8,128)(2,1)}), bf16[512,16384]{1,0:T(8,128)(2,1)}) %all-gather.2.cloned.1.call-update) | async-done | bytes 16777232 | tf_op jit(solution)/shard_map/all_gather | solution.py:30
  125.4 16.4 %fusion.5 = f32[512,512]{1,0:T(8,128)S(1)} fusion(bf16[512,16384]{1,0:T(8,128)(2,1)} %all-gather.2.cloned.1.call-done, bf16[16384,512]{1,0:T(8,128)(2,1)} %param.5), kind=kOutput, calls=%fused_computation.10 | convolution fusion | flops 8589934592 | bytes 34603008 | tf_op jit(solution)/shard_map/dot_general | solution.py:29
  141.9 0.3 all_to_all.18
  142.2 28.3 %all_to_all.25 = f32[128,4,512]{2,1,0:T(4,128)S(1)} all-to-all(f32[128,4,512]{2,1,0:T(4,128)S(1)} %all_to_all.18), channel_id=1, replica_groups=mesh['grp'=16,'tp'=8] {'grp','tp'}, dimensions={0} | all-to-all | bytes 2097152 | tf_op jit(solution)/shard_map/all_to_all | solution.py:34
  170.4 0.7 reduce_max.9
  171.1 0.7 fusion.1
  171.8 1.2 subtract_subtract_fusion
  (2 shorter events, 0.0 us)
Async XLA Ops:
  6.5 118.9 %all-gather.2.cloned.1.call-start = ((), (), s32[]{:S(2)}) async-start(), calls=%async_computation.2 | async-start | bytes 17825792 | tf_op jit(solution)/shard_map/all_gather | solution.py:30
Sparse Core Ops, SparseCore 0:
  32.8 92.5 all-gather.1
where the time goes:
time: 180 us
  waiting for transfers between devices  92.8 us (52%)
  blocking collectives  50.8 us (28%)
  matrix products  16.4 us (9%)
  between operations  13.4 us (7%)
  other arithmetic  4.83 us (3%)
    all_gather x1, waiting for transfers between devices, on_device(): lax.all_gather(group_block, 'grp', axis=0, tiled=True)  92.8 us
    all_to_all x1, blocking collectives, on_device(): lax.all_to_all(logits, ('grp', 'tp'), split_axis=0, concat_axis=1, tiled=...  28.3 us
    all_to_all x1, blocking collectives, sent_to_all(): lax.all_to_all(jnp.broadcast_to(array[None], (count, *array.shape)), axis...  22.5 us
    dot_general x1, matrix products, on_device(): jnp.dot(lax.all_gather(group_block, 'grp', axis=0, tiled=True), head, pre...  16.4 us
  transfers between devices with their start and end apart: 1, of which 1 were waited for; matrix products, arithmetic and copies ran while one was open for 0% of the time, Pallas kernels for 0%

commit v1 on v0

v1 whole, which is shorter than its diff:
```python
import jax
import jax.numpy as jnp
from jax import lax
from jax.experimental import pallas as pl
from jax.experimental.pallas import tpu as pltpu
from jax.sharding import PartitionSpec as P

MESH = pl.DeviceIdType.MESH
D, V, TOK = 16384, 512, 4
QUARTER = D // 4
TILE = 128
PARTS = ((0, 11, 6), (11, 22, 17), (22, 32, 27))
ORDERS = ((0, 1, 2), (1, 2, 0), (2, 0, 1))


def position():
    grp, tp = lax.axis_index("grp"), lax.axis_index("tp")
    return (tp // 2, (tp % 2) * 2 + (grp // 2) % 2, grp // 4), grp % 2


def device(at, core):
    x, y, z = at
    return ((z * 2 + y % 2) * 2 + core, x * 2 + y // 2)


def moved(at, axis, step):
    at = list(at)
    at[axis] = (at[axis] + step + 4) % 4
    return tuple(at)


def gather_matmul(hidden_ref, gain_ref, head_ref, out_ref, norm, piece, units, head, send, recv, local):
    me, core = position()
    partner = (me[0] + 1 - 2 * (me[0] % 2), me[1], me[2])
    member = (me[0] % 2) * 2 + core
    heads = []
    for quarter in range(4):
        copy = pltpu.make_async_copy(
            head_ref.at[pl.ds(quarter * QUARTER, QUARTER)], head.at[quarter], local.at[quarter]
        )
        copy.start()
        heads.append(copy)

    barrier = pltpu.get_barrier_semaphore()
    greeted = [device(moved(me, axis, step), core) for axis in range(3) for step in (1, -1)]
    greeted += [device(me, 1 - core), device(partner, 1 - core)]
    for other in greeted:
        pl.semaphore_signal(barrier, inc=1, device_id=other, device_id_type=MESH)

    values = hidden_ref[...].astype(jnp.float32)
    scale = lax.rsqrt(jnp.mean(values * values, axis=-1, keepdims=True) + 1e-05)
    for quarter in range(4):
        columns = slice(quarter * QUARTER, (quarter + 1) * QUARTER)
        normed = hidden_ref[:, columns].astype(jnp.float32) * scale * gain_ref[:, columns]
        wide = QUARTER // 4
        stacked = jnp.concatenate([normed[:, j * wide : (j + 1) * wide] for j in range(4)], axis=0)
        norm[quarter] = stacked.astype(jnp.bfloat16)
    pl.semaphore_wait(barrier, len(greeted))

    sent = []
    count = [0]

    def start(source, target, other):
        event = count[0]
        count[0] += 1
        copy = pltpu.make_async_remote_copy(
            source, target, send.at[event], recv.at[event], device_id=other, device_id_type=MESH
        )
        copy.start()
        sent.append(copy)
        return event

    swaps = []
    for relation in (1, 2, 3):
        i, c = member // 2, core
        i = 1 - i if relation & 2 else i
        c = 1 - c if relation & 1 else c
        other = device(partner if relation & 2 else me, c)
        event = start(norm.at[i * 2 + c], piece.at[member], other)
        swaps.append((event, i * 2 + c, other))
    mine = norm[member]
    piece[member] = mine
    for event, theirs, other in swaps:
        pltpu.make_async_remote_copy(
            norm.at[theirs], piece.at[theirs], send.at[event], recv.at[event], device_id=other, device_id_type=MESH
        ).wait_recv()
    wide = QUARTER // 4
    for j in range(4):
        rows = [piece[s].astype(jnp.float32)[j * 4 : j * 4 + 4] for s in range(4)]
        units[me[0], me[1], me[2], core, :, j * wide : (j + 1) * wide] = jnp.concatenate(rows, axis=0).astype(jnp.bfloat16)

    def view(part, at, of, span):
        order = ORDERS[part]
        index = [None] * 3
        for axis, value in zip(order, at):
            index[axis] = pl.ds(0, 4) if value is None else value
        first, last, middle = PARTS[part]
        low, high = {0: (first, middle), 1: (middle, last), 2: (first, last)}[span]
        return units.at[index[0], index[1], index[2], of, :, pl.ds(low * TILE, (high - low) * TILE)]

    sibling = device(me, 1 - core)

    def route(part):
        order = ORDERS[part]
        a, b, c = (me[axis] for axis in order)
        near = {(k, s): device(moved(me, order[k], s), core) for k in range(3) for s in (1, -1)}

        def at(da, db, dc):
            return (None if da is None else (a + da + 4) % 4, (b + db + 4) % 4, (c + dc + 4) % 4)

        def push(k, step, where, span=2):
            ref = view(part, at(*where), core, span)
            return start(ref, ref, near[k, step])

        def arrived(event, where, span=2, of=core, other=sibling):
            ref = view(part, at(*where), of, span)
            pltpu.make_async_remote_copy(
                ref, ref, send.at[event], recv.at[event], device_id=other, device_id_type=MESH
            ).wait_recv()

        across = {}

        def share(db, dc):
            ref = view(part, at(None, db, dc), core, 2)
            across[db, dc] = start(ref, ref, sibling)

        first = {s: push(0, s, (0, 0, 0)) for s in (1, -1)}
        line = {(0, s): push(1, s, (0, 0, 0)) for s in (1, -1)}
        yield
        second = {}
        for s, span in ((1, 0), (-1, 1)):
            arrived(first[s], (-s, 0, 0))
            second[s] = push(0, s, (-s, 0, 0), span)
            for t in (1, -1):
                line[-s, t] = push(1, t, (-s, 0, 0))
        yield
        for s, span in ((1, 0), (-1, 1)):
            arrived(second[s], (2, 0, 0), span)
        for t in (1, -1):
            line[2, t] = push(1, t, (2, 0, 0))
        plane = {(0, t): push(2, t, (None, 0, 0)) for t in (1, -1)}
        share(0, 0)
        yield
        onward = {}
        for da, t in ((0, 1), (0, -1), (-1, 1), (-1, -1), (1, 1), (1, -1), (2, 1), (2, -1)):
            arrived(line[da, t], (da, -t, 0))
            if (t == 1) == (da in (0, -1)):
                onward[da] = (push(1, t, (da, -t, 0)), t)
        for db in (-1, 1):
            for t in (1, -1):
                plane[db, t] = push(2, t, (None, db, 0))
            share(db, 0)
        yield
        for da in (0, -1, 1, 2):
            arrived(onward[da][0], (da, 2, 0))
        for t in (1, -1):
            plane[2, t] = push(2, t, (None, 2, 0))
        share(2, 0)
        yield
        last = {}
        for db in (0, -1, 1, 2):
            for t in (1, -1):
                arrived(plane[db, t], (None, db, -t))
                if (t == 1) == (db in (0, -1)):
                    last[db] = push(2, t, (None, db, -t))
                share(db, -t)
            yield
        for db in (0, 1, -1, 2):
            arrived(last[db], (None, db, 2))
            share(db, 2)
        yield
        yield lambda dc: [
            arrived(across[db, dc], (None, db, dc), of=1 - core) for db in (0, -1, 1, 2)
        ]

    def multiply(part, dc, first):
        axis = ORDERS[part][2]
        at = (me[axis] + dc + 4) % 4
        low, high, _ = PARTS[part]
        wide = (high - low) * TILE
        columns = pl.ds(low * TILE, wide)
        if axis == 0:
            for of in (0, 1):
                rows = units[at, :, :, of, :, columns].reshape(256, wide)
                weights = head[(at % 2) * 2 + of, columns]
                product = jnp.dot(rows, weights, preferred_element_type=jnp.float32).reshape(1, 4, 4, 16, V)
                out_ref[pl.ds(at // 2, 1)] += product
            return
        for i in (0, 1):
            for of in (0, 1):
                if axis == 1:
                    rows = jnp.concatenate([units[2 * h + i, at, :, of, :, columns].reshape(64, wide) for h in (0, 1)], axis=0)
                else:
                    rows = jnp.concatenate([units[2 * h + i, :, at, of, :, columns].reshape(64, wide) for h in (0, 1)], axis=0)
                weights = head[i * 2 + of, columns]
                product = jnp.dot(rows, weights, preferred_element_type=jnp.float32).reshape(2, 4, 16, V)
                if axis == 1:
                    out_ref[:, at] += product
                else:
                    out_ref[:, :, at] += product

    routes = [route(part) for part in range(3)]
    for _ in range(5):
        for r in routes:
            next(r)
    out_ref[...] = jnp.zeros_like(out_ref)
    for _ in range(4):
        for r in routes:
            next(r)
    for r in routes:
        next(r)
    fetched = [next(r) for r in routes]
    for copy in heads:
        copy.wait()
    for part in range(3):
        for dc in (0, -1, 1, 2):
            fetched[part](dc)
            multiply(part, dc, False)
    for copy in sent:
        copy.wait_send()


EVENTS = 3 + 3 * 44


def on_device(hidden, gain, head):
    logits = pl.pallas_call(
        gather_matmul,
        out_shape=jax.ShapeDtypeStruct((2, 4, 4, 16, V), jnp.float32),
        in_specs=[
            pl.BlockSpec(memory_space=pltpu.VMEM),
            pl.BlockSpec(memory_space=pltpu.VMEM),
            pl.BlockSpec(memory_space=pl.ANY),
        ],
        out_specs=pl.BlockSpec(memory_space=pltpu.VMEM),
        scratch_shapes=[
            pltpu.VMEM((4, 16, QUARTER // 4), jnp.bfloat16),
            pltpu.VMEM((4, 16, QUARTER // 4), jnp.bfloat16),
            pltpu.VMEM((4, 4, 4, 2, 16, QUARTER), jnp.bfloat16),
            pltpu.VMEM((4, QUARTER, V), jnp.bfloat16),
            pltpu.SemaphoreType.DMA((EVENTS,)),
            pltpu.SemaphoreType.DMA((EVENTS,)),
            pltpu.SemaphoreType.DMA((4,)),
        ],
        compiler_params=pltpu.CompilerParams(
            collective_id=0, has_side_effects=True, vmem_limit_bytes=56 * 2**20
        ),
        cost_estimate=pl.CostEstimate(
            flops=2 * 512 * D * V, bytes_accessed=D * V * 2, transcendentals=0
        ),
    )(hidden, gain.reshape(1, D), head)
    pieces = logits.reshape(2, 2, 2, 4, 2, 2, TOK, V).transpose(3, 2, 5, 0, 4, 1, 6, 7)
    pieces = pieces.reshape(128, TOK, V)
    owned = lax.all_to_all(pieces, ("grp", "tp"), split_axis=0, concat_axis=0, tiled=True)
    owned = owned.transpose(1, 0, 2).reshape(TOK, 128 * V)
    top = jnp.max(owned, axis=-1, keepdims=True)
    total = jnp.sum(jnp.exp(owned - top), axis=-1, keepdims=True)
    return owned - top - jnp.log(total)


def solution(mesh):
    return jax.shard_map(
        on_device,
        mesh=mesh,
        in_specs=(P(("grp", "tp"), None), P(), P(None, ("grp", "tp"))),
        out_specs=P(("grp", "tp"), None),
        check_vma=False,
    )
```

time: 180 us -> 92.3 us (0.51)
  waiting for transfers between devices: 92.8 us -> 0 us
  Pallas kernels: 0 us -> 59.5 us
  blocking collectives: 50.8 us -> 28.3 us
  matrix products: 16.4 us -> 0 us
  between operations: 13.4 us -> 0.02 us
  other arithmetic: 4.83 us -> 2.62 us
    all_gather x1 -> x0, waiting for transfers between devices: 92.8 us -> none  [on_device(): lax.all_gather(group_block, 'grp', axis=0, tiled=True)]
    pallas_call x0 -> x1, Pallas kernels: none -> 59.5 us  [on_device(): pl.pallas_call(gather_matmul, out_shape=jax.ShapeDtypeStruct((2, 4, 4, 16...]
    all_to_all x2 -> x1, blocking collectives: 50.8 us -> 28.3 us  [on_device(): lax.all_to_all(pieces, ('grp', 'tp'), split_axis=0, concat_axis=0, tiled=...]
    dot_general x1 -> x0, matrix products: 16.4 us -> none  [on_device(): jnp.dot(lax.all_gather(group_block, 'grp', axis=0, tiled=True), head, pre...]
  transfers between devices with their start and end apart: 1 -> 0, of which waited for: 1 -> 0; matrix products, arithmetic and copies ran while one was open for 0% -> 0% of each run, Pallas kernels for 0% -> 0%
where the time goes in v1:
time: 92.3 us; the launch traced here: 92.1 us
  Pallas kernels  59.5 us (64%)
  blocking collectives  28.3 us (31%)
  other arithmetic  2.62 us (3%)
  local copies, waits for them, and re-layouts  1.69 us (2%)
    pallas_call x1, Pallas kernels, on_device(): pl.pallas_call(gather_matmul, out_shape=jax.ShapeDtypeStruct((2, 4, 4, 16...  59.5 us
    all_to_all x1, blocking collectives, on_device(): lax.all_to_all(pieces, ('grp', 'tp'), split_axis=0, concat_axis=0, tiled=...  28.3 us

profile of v1, /device:TPU:1, one launch (start us, length us, event | category | flops | bytes accessed | tf_op | source)
XLA Modules:
  0.0 92.1 jit_solution(17117293175360542261)
XLA Ops:
  0.0 59.5 %shard_map.37 = f32[2,4,4,16,512]{4,3,2,1,0:T(8,128)} custom-call(bf16[4,16384]{1,0:T(4,128)(2,1)} %hidden_ref.1, f32[1,16384]{1,0:T(1,128)} %bitcast.16, bf16[16384,512]{1,0:T(8,128)(2,1)} %head_ref.1), custom_call_target="tpu_custom_call" | custom-call | flops 8589934592 | bytes 16777216 | tf_op jit(solution)/shard_map/pallas_call | solution.py:227
  59.5 1.5 %reshape.22 = f32[2,2,2,4,2,2,4,512]{7,6,5,4,3,2,1,0:T(4,128)S(1)} reshape(f32[2,4,4,16,512]{4,3,2,1,0:T(8,128)} %shard_map.37) | data formatting | bytes 2097152 | tf_op jit(solution)/shard_map/reshape | solution.py:252
  61.0 0.2 copy.4
  61.2 28.3 %all_to_all.5 = f32[128,4,512]{2,1,0:T(4,128)S(1)} all-to-all(f32[128,4,512]{2,1,0:T(4,128)S(1)} %bitcast.15), channel_id=1, replica_groups=mesh['grp'=16,'tp'=8] {'grp','tp'}, dimensions={0} | all-to-all | bytes 2097152 | tf_op jit(solution)/shard_map/all_to_all | solution.py:254
  89.5 0.7 reduce_max.9
  90.2 0.7 fusion.1
  90.9 1.2 %subtract_subtract_fusion = f32[4,65536]{1,0:T(4,128)} fusion(f32[4,65536]{1,0:T(4,128)S(1)} %bitcast.14, f32[4]{0:T(128)S(1)} %log.8, f32[4]{0:T(128)S(1)} %reduce_max.9), kind=kLoop, calls=%fused_computation.3 | loop fusion | flops 524288 | bytes 2097184 | tf_op jit(solution)/shard_map/sub | solution.py:258
  (1 shorter events, 0.0 us)

commit v2 on v1

--- a/solution.py
+++ b/solution.py
@@ -10,6 +10,7 @@
 QUARTER = D // 4
 TILE = 128
 PARTS = ((0, 11, 6), (11, 22, 17), (22, 32, 27))
+STEEP, FLOOR, LOWEST = 17.5, 8.0, 125.0
 ORDERS = ((0, 1, 2), (1, 2, 0), (2, 0, 1))
 
 
@@ -29,7 +30,19 @@
     return tuple(at)
 
 
-def gather_matmul(hidden_ref, gain_ref, head_ref, out_ref, norm, piece, units, head, send, recv, local):
+def encode(d):
+    size = jnp.exp2(STEEP * jnp.log2(1.0 + jnp.abs(d) * (1.0 / FLOOR)) - LOWEST)
+    return jnp.where(d < 0, -size, size).astype(jnp.bfloat16).astype(jnp.float32)
+
+
+def decode(v):
+    size = FLOOR * (jnp.exp2((jnp.log2(jnp.abs(v)) + LOWEST) * (1.0 / STEEP)) - 1.0)
+    return jnp.where(v < 0, -size, size)
+
+
+def gather_matmul(
+    hidden_ref, gain_ref, head_ref, out_ref, norm, piece, units, head, acc, codes, got, logits, send, recv, local, spread
+):
     me, core = position()
     partner = (me[0] + 1 - 2 * (me[0] % 2), me[1], me[2])
     member = (me[0] % 2) * 2 + core
@@ -99,6 +112,7 @@
         return units.at[index[0], index[1], index[2], of, :, pl.ds(low * TILE, (high - low) * TILE)]
 
     sibling = device(me, 1 - core)
+    arrivals = {}
 
     def route(part):
         order = ORDERS[part]
@@ -123,6 +137,8 @@
         def share(db, dc):
             ref = view(part, at(None, db, dc), core, 2)
             across[db, dc] = start(ref, ref, sibling)
+
+        arrivals[part] = lambda db, dc: arrived(across[db, dc], (None, db, dc), of=1 - core)
 
         first = {s: push(0, s, (0, 0, 0)) for s in (1, -1)}
         line = {(0, s): push(1, s, (0, 0, 0)) for s in (1, -1)}
@@ -168,12 +184,9 @@
         for db in (0, 1, -1, 2):
             arrived(last[db], (None, db, 2))
             share(db, 2)
-        yield
-        yield lambda dc: [
-            arrived(across[db, dc], (None, db, dc), of=1 - core) for db in (0, -1, 1, 2)
-        ]
-
-    def multiply(part, dc, first):
+            yield
+
+    def multiply(part, dc):
         axis = ORDERS[part][2]
         at = (me[axis] + dc + 4) % 4
         low, high, _ = PARTS[part]
@@ -184,7 +197,7 @@
                 rows = units[at, :, :, of, :, columns].reshape(256, wide)
                 weights = head[(at % 2) * 2 + of, columns]
                 product = jnp.dot(rows, weights, preferred_element_type=jnp.float32).reshape(1, 4, 4, 16, V)
-                out_ref[pl.ds(at // 2, 1)] += product
+                acc[pl.ds(at // 2, 1)] += product
             return
         for i in (0, 1):
             for of in (0, 1):
@@ -195,38 +208,124 @@
                 weights = head[i * 2 + of, columns]
                 product = jnp.dot(rows, weights, preferred_element_type=jnp.float32).reshape(2, 4, 16, V)
                 if axis == 1:
-                    out_ref[:, at] += product
+                    acc[:, at] += product
                 else:
-                    out_ref[:, :, at] += product
+                    acc[:, :, at] += product
 
     routes = [route(part) for part in range(3)]
-    for _ in range(5):
-        for r in routes:
-            next(r)
-    out_ref[...] = jnp.zeros_like(out_ref)
-    for _ in range(4):
-        for r in routes:
-            next(r)
-    for r in routes:
-        next(r)
-    fetched = [next(r) for r in routes]
+
+    def advance(steps=1):
+        for _ in range(steps):
+            for r in routes:
+                next(r)
+
+    advance(4)
+    acc[...] = jnp.zeros_like(acc)
     for copy in heads:
         copy.wait()
+    advance(2)
+
+    def sibling_plane(part, dc):
+        for db in (0, -1, 1, 2):
+            arrivals[part](db, dc)
+
+    for step in range(3):
+        sibling_plane(step, 0)
+        multiply(step, 0)
+        advance(1)
     for part in range(3):
-        for dc in (0, -1, 1, 2):
-            fetched[part](dc)
-            multiply(part, dc, False)
+        for dc in (-1, 1):
+            sibling_plane(part, dc)
+            multiply(part, dc)
+    advance(4)
+    for part in range(3):
+        sibling_plane(part, 2)
+        multiply(part, 2)
+
+    grp, tp = lax.axis_index("grp"), lax.axis_index("tp")
+    here = grp * 8 + tp
+
+    def messages(xh, y, z):
+        rows = acc[xh, y, z]
+        anchor = decode(encode(rows[:, :1]))
+        lane = lax.broadcasted_iota(jnp.int32, rows.shape, 1)
+        coded = encode(jnp.where(lane == 0, rows, rows - anchor))
+        for m in range(4):
+            yield m, jnp.concatenate(
+                [coded[4 * m : 4 * m + 4, TILE * j : TILE * (j + 1)] for j in range(4)], axis=0
+            ).astype(jnp.bfloat16)
+
+    def deliver(slot, i, c, xh, y, z):
+        pltpu.make_async_remote_copy(
+            codes.at[slot], got.at[here], spread.at[0], spread.at[1],
+            device_id=device((2 * xh + i, y, z), c), device_id_type=MESH,
+        ).start()
+
+    def emit(k, _):
+        xh, y, z = (me[0] // 2 + k) % 2, (me[1] + k // 2) % 4, (me[2] + k // 8) % 4
+        for m, message in messages(xh, y, z):
+            codes[k * 4 + m] = message
+            deliver(k * 4 + m, m // 2, m % 2, xh, y, z)
+        return 0
+
+    lax.fori_loop(1, 32, emit, 0)
+    xh = me[0] // 2
+    for m, message in messages(xh, me[1], me[2]):
+        codes[m] = message
+    got[here] = codes[member]
+    for relation in (1, 2, 3):
+        i = 1 - member // 2 if relation & 2 else member // 2
+        c = 1 - core if relation & 1 else core
+        deliver(i * 2 + c, i, c, xh, me[1], me[2])
+    pltpu.make_async_remote_copy(
+        codes.at[pl.ds(0, 127)], got.at[pl.ds(0, 127)], spread.at[0], spread.at[1],
+        device_id=sibling, device_id_type=MESH,
+    ).wait()
     for copy in sent:
         copy.wait_send()
 
+    def four(rows):
+        return jnp.concatenate([rows] * 4, axis=0)
+
+    first_lane = lax.broadcasted_iota(jnp.int32, (16, TILE), 1) == 0
+    first = first_lane & (lax.broadcasted_iota(jnp.int32, (16, TILE), 0) < 4)
+
+    def open_message(s, top):
+        d = decode(got[s].astype(jnp.float32))
+        anchor = four(d[:4, :1])
+        values = jnp.where(first, d, d + anchor)
+        logits[s] = values
+        return jnp.maximum(top, values)
+
+    def by_token(rows, combine, reduce):
+        each = reduce(rows, axis=1, keepdims=True)
+        return combine(combine(each[:4], each[4:8]), combine(each[8:12], each[12:]))
+
+    top = lax.fori_loop(0, 128, open_message, jnp.full((16, TILE), -jnp.inf, jnp.float32), unroll=4)
+    top = by_token(top, jnp.maximum, jnp.max)
+    top_rows = jnp.broadcast_to(four(top), (16, TILE))
+    total = lax.fori_loop(
+        0, 128, lambda s, t: t + jnp.exp(logits[s] - top_rows), jnp.zeros((16, TILE), jnp.float32), unroll=8
+    )
+    total = by_token(total, jnp.add, jnp.sum)
+    top_row = jnp.broadcast_to(top, (4, TILE))
+    log_row = jnp.broadcast_to(jnp.log(total), (4, TILE))
+
+    def finish(s, _):
+        for j in range(4):
+            out_ref[s, :, TILE * j : TILE * (j + 1)] = logits[s, 4 * j : 4 * j + 4] - top_row - log_row
+        return 0
+
+    lax.fori_loop(0, 128, finish, 0, unroll=8)
+
 
 EVENTS = 3 + 3 * 44
 
 
 def on_device(hidden, gain, head):
-    logits = pl.pallas_call(
+    log_probs = pl.pallas_call(
         gather_matmul,
-        out_shape=jax.ShapeDtypeStruct((2, 4, 4, 16, V), jnp.float32),
+        out_shape=jax.ShapeDtypeStruct((128, TOK, V), jnp.float32),
         in_specs=[
             pl.BlockSpec(memory_space=pltpu.VMEM),
             pl.BlockSpec(memory_space=pltpu.VMEM),
@@ -238,9 +337,14 @@
             pltpu.VMEM((4, 16, QUARTER // 4), jnp.bfloat16),
             pltpu.VMEM((4, 4, 4, 2, 16, QUARTER), jnp.bfloat16),
             pltpu.VMEM((4, QUARTER, V), jnp.bfloat16),
+            pltpu.VMEM((2, 4, 4, 16, V), jnp.float32),
+            pltpu.VMEM((128, 16, TILE), jnp.bfloat16),
+            pltpu.VMEM((128, 16, TILE), jnp.bfloat16),
+            pltpu.VMEM((128, 16, TILE), jnp.float32),
             pltpu.SemaphoreType.DMA((EVENTS,)),
             pltpu.SemaphoreType.DMA((EVENTS,)),
             pltpu.SemaphoreType.DMA((4,)),
+            pltpu.SemaphoreType.DMA((2,)),
         ],
         compiler_params=pltpu.CompilerParams(
             collective_id=0, has_side_effects=True, vmem_limit_bytes=56 * 2**20
@@ -249,13 +353,7 @@
             flops=2 * 512 * D * V, bytes_accessed=D * V * 2, transcendentals=0
         ),
     )(hidden, gain.reshape(1, D), head)
-    pieces = logits.reshape(2, 2, 2, 4, 2, 2, TOK, V).transpose(3, 2, 5, 0, 4, 1, 6, 7)
-    pieces = pieces.reshape(128, TOK, V)
-    owned = lax.all_to_all(pieces, ("grp", "tp"), split_axis=0, concat_axis=0, tiled=True)
-    owned = owned.transpose(1, 0, 2).reshape(TOK, 128 * V)
-    top = jnp.max(owned, axis=-1, keepdims=True)
-    total = jnp.sum(jnp.exp(owned - top), axis=-1, keepdims=True)
-    return owned - top - jnp.log(total)
+    return log_probs.transpose(1, 0, 2).reshape(TOK, 128 * V)
 
 
 def solution(mesh):

time: 92.3 us -> 75.2 us (0.81)
  blocking collectives: 28.3 us -> 0 us
  Pallas kernels: 59.5 us -> 72.8 us
  other arithmetic: 2.62 us -> 0 us
    all_to_all x1 -> x0, blocking collectives: 28.3 us -> none  [on_device(): lax.all_to_all(pieces, ('grp', 'tp'), split_axis=0, concat_axis=0, tiled=...]
    pallas_call x1, Pallas kernels: 59.5 us -> 72.8 us  [on_device(): pl.pallas_call(gather_matmul, out_shape=jax.ShapeDtypeStruct((128, TOK, V...]
    unnamed x0 -> x1, local copies, waits for them, and re-layouts: none -> 2.26 us
    reshape x2 -> x0, local copies, waits for them, and re-layouts: 1.68 us -> none  [on_device(): logits.reshape(2, 2, 2, 4, 2, 2, TOK, V).transpose(3, 2, 5, 0, 4, 1, 6, 7)]
    sub x1 -> x0, other arithmetic: 1.23 us -> none  [on_device(): return owned - top - jnp.log(total)]
where the time goes in v2:
time: 75.2 us; the launch traced here: 75 us
  Pallas kernels  72.8 us (97%)
  local copies, waits for them, and re-layouts  2.26 us (3%)
    pallas_call x1, Pallas kernels, on_device(): pl.pallas_call(gather_matmul, out_shape=jax.ShapeDtypeStruct((128, TOK, V...  72.8 us
    unnamed x1, local copies, waits for them, and re-layouts  2.26 us

profile of v2, /device:TPU:1, one launch (start us, length us, event | category | flops | bytes accessed | tf_op | source)
XLA Modules:
  0.0 75.0 jit_solution(2379634775292149876)
XLA Ops:
  0.0 72.8 %shard_map.37 = f32[128,4,512]{2,1,0:T(4,128)} custom-call(bf16[4,16384]{1,0:T(4,128)(2,1)} %hidden_ref.1, f32[1,16384]{1,0:T(1,128)} %bitcast.5, bf16[16384,512]{1,0:T(8,128)(2,1)} %head_ref.1), custom_call_target="tpu_custom_call" | custom-call | flops 8589934592 | bytes 16777216 | tf_op jit(solution)/shard_map/pallas_call | solution.py:326
  72.8 2.3 %copy.5 = f32[4,65536]{1,0:T(4,128)} copy(f32[4,65536]{1,0:T(4,128)} %bitcast.4) | data formatting | bytes 2097152

commit v3 on v0

v3 whole, which is shorter than its diff:
```python
import jax
import jax.numpy as jnp
from jax import lax
from jax.experimental import pallas as pl
from jax.experimental.pallas import tpu as pltpu
from jax.sharding import PartitionSpec as P

MESH = pl.DeviceIdType.MESH
D, V, TOK = 16384, 512, 4
QUARTER = D // 4
TILE = 128
PARTS = ((0, 11, 6), (11, 22, 17), (22, 32, 27))
ORDERS = ((0, 1, 2), (1, 2, 0), (2, 0, 1))
STEEP, FLOOR, LOWEST = 17.5, 8.0, 125.0
EVENTS = 1 + 3 * 39


def position():
    grp, tp = lax.axis_index("grp"), lax.axis_index("tp")
    return (tp // 2, (tp % 2) * 2 + (grp // 2) % 2, grp // 4), grp % 2


def device(at, core):
    x, y, z = at
    return ((z * 2 + y % 2) * 2 + core, x * 2 + y // 2)


def moved(at, axis, step):
    at = list(at)
    at[axis] = (at[axis] + step + 4) % 4
    return tuple(at)


def encode(d):
    size = jnp.exp2(STEEP * jnp.log2(1.0 + jnp.abs(d) * (1.0 / FLOOR)) - LOWEST)
    return jnp.where(d < 0, -size, size).astype(jnp.bfloat16).astype(jnp.float32)


def decode(v):
    size = FLOOR * (jnp.exp2((jnp.log2(jnp.abs(v)) + LOWEST) * (1.0 / STEEP)) - 1.0)
    return jnp.where(v < 0, -size, size)


def kernel(
    hidden_ref, gain_ref, head_ref, out_ref, norm, piece, units, head, acc, codes, got, logits, send, recv, local, spread
):
    me, core = position()
    sibling = device(me, 1 - core)
    heads = []
    for quarter in range(4):
        copy = pltpu.make_async_copy(
            head_ref.at[pl.ds(quarter * QUARTER, QUARTER)], head.at[quarter], local.at[quarter]
        )
        copy.start()
        heads.append(copy)

    barrier = pltpu.get_barrier_semaphore()
    greeted = [device(moved(me, axis, step), core) for axis in range(3) for step in (1, -1, 2)]
    greeted.append(sibling)
    for other in greeted:
        pl.semaphore_signal(barrier, inc=1, device_id=other, device_id_type=MESH)

    values = hidden_ref[...].astype(jnp.float32)
    scale = lax.rsqrt(jnp.mean(values * values, axis=-1, keepdims=True) + 1e-05)
    wide = D // 8
    for half in range(2):
        rows = []
        for j in range(4):
            columns = slice(half * 2 * QUARTER + j * wide, half * 2 * QUARTER + (j + 1) * wide)
            rows.append(hidden_ref[:, columns].astype(jnp.float32) * scale * gain_ref[:, columns])
        norm[half] = jnp.concatenate(rows, axis=0).astype(jnp.bfloat16)
    pl.semaphore_wait(barrier, len(greeted))

    sent = {}
    count = [0]

    def start(source, target, other):
        event = count[0]
        count[0] += 1
        copy = pltpu.make_async_remote_copy(
            source, target, send.at[event], recv.at[event], device_id=other, device_id_type=MESH
        )
        copy.start()
        sent[event] = copy
        return event

    event = start(norm.at[1 - core], piece.at[core], sibling)
    piece[core] = norm[core]
    pltpu.make_async_remote_copy(
        norm.at[core], piece.at[1 - core], send.at[event], recv.at[event], device_id=sibling, device_id_type=MESH
    ).wait_recv()
    both = [piece[s].astype(jnp.float32) for s in (0, 1)]
    for j in (0, 1):
        rows = [both[s][8 * h + 4 * j : 8 * h + 4 * j + 4] for h in (0, 1) for s in (0, 1)]
        units[me[0], me[1], me[2], core, :, j * wide : (j + 1) * wide] = jnp.concatenate(rows, axis=0).astype(jnp.bfloat16)

    def view(part, at, of, span):
        order = ORDERS[part]
        index = [None] * 3
        for axis, value in zip(order, at):
            index[axis] = pl.ds(0, 4) if value is None else value
        first, last, middle = PARTS[part]
        low, high = {0: (first, middle), 1: (middle, last), 2: (first, last)}[span]
        return units.at[index[0], index[1], index[2], of, :, pl.ds(low * TILE, (high - low) * TILE)]

    class Route:
        def __init__(self, part):
            self.part = part
            order = ORDERS[part]
            self.at = [me[axis] for axis in order]
            self.near = {(k, s): device(moved(me, order[k], s), core) for k in range(3) for s in (1, -1, 2)}
            self.events = {}

        def where(self, da, db, dc):
            a, b, c = self.at
            return (None if da is None else (a + da + 4) % 4, (b + db + 4) % 4, (c + dc + 4) % 4)

        def push(self, name, k, step, where, span=2):
            ref = view(self.part, self.where(*where), core, span)
            self.events[name] = start(ref, ref, self.near[k, step])

        def share(self, db, dc):
            ref = view(self.part, self.where(None, db, dc), core, 2)
            self.events["share", db, dc] = start(ref, ref, sibling)

        def arrived(self, name, where, span=2, of=core):
            ref = view(self.part, self.where(*where), of, span)
            event = self.events[name]
            pltpu.make_async_remote_copy(
                ref, ref, send.at[event], recv.at[event], device_id=sibling, device_id_type=MESH
            ).wait_recv()

    routes = [Route(part) for part in range(3)]
    for r in routes:
        for s in (1, -1, 2):
            r.push(("a", s), 0, s, (0, 0, 0))
    acc[...] = jnp.zeros_like(acc)
    for r in routes:
        for s in (1, -1, 2):
            r.arrived(("a", s), (-s, 0, 0))
        for s in (1, -1):
            r.push(("b", s), 1, s, (None, 0, 0))
    for r in routes:
        r.share(0, 0)
    for r in routes:
        for s in (1, -1):
            r.push(("c", 0, s), 2, s, (None, 0, 0))
    for r in routes:
        for s, span in ((1, 0), (-1, 1)):
            r.arrived(("b", s), (None, -s, 0))
            r.push(("bb", s), 1, s, (None, -s, 0), span)
    for db in (-1, 1):
        for r in routes:
            for s in (1, -1):
                r.push(("c", db, s), 2, s, (None, db, 0))
            r.share(db, 0)
    for r in routes:
        for s, span in ((1, 0), (-1, 1)):
            r.arrived(("bb", s), (None, 2, 0), span)
        for s in (1, -1):
            r.push(("c", 2, s), 2, s, (None, 2, 0))
        r.share(2, 0)

    def onward(db):
        for r in routes:
            for s, span in ((1, 0), (-1, 1)):
                r.arrived(("c", db, s), (None, db, -s))
                r.push(("cc", db, s), 2, s, (None, db, -s), span)
            for s in (1, -1):
                r.share(db, -s)

    def last(db):
        for r in routes:
            for s, span in ((1, 0), (-1, 1)):
                r.arrived(("cc", db, s), (None, db, 2), span)
            r.share(db, 2)

    def multiply(part, *planes):
        r = routes[part]
        axis = ORDERS[part][2]
        at = [r.where(0, 0, dc)[2] for dc in planes]
        for dc in planes:
            for db in (0, -1, 1, 2):
                r.arrived(("share", db, dc), (None, db, dc), of=1 - core)
        low, high, _ = PARTS[part]
        columns = pl.ds(low * TILE, (high - low) * TILE)
        for of in (0, 1):
            for h in (0, 1):
                rows = []
                for p in at:
                    index = [slice(None)] * 3
                    index[axis] = p
                    rows.append(units[(*index, of, slice(8 * h, 8 * h + 8), columns)].reshape(128, (high - low) * TILE))
                product = jnp.dot(
                    jnp.concatenate(rows, axis=0) if len(rows) > 1 else rows[0],
                    head[of * 2 + h, columns],
                    preferred_element_type=jnp.float32,
                )
                for n, p in enumerate(at):
                    index = [slice(None)] * 3
                    index[axis] = p
                    acc[tuple(index)] += product[n * 128 : (n + 1) * 128].reshape(4, 4, 8, V)

    grp, tp = lax.axis_index("grp"), lax.axis_index("tp")
    here = grp * 8 + tp

    def deliver(slot, s, at):
        pltpu.make_async_remote_copy(
            codes.at[slot, s], got.at[here], spread.at[0], spread.at[1], device_id=device(at, s), device_id_type=MESH
        ).start()

    def chip(dx, dy, dz):
        return tuple(lax.rem(axis + d, 4) for axis, d in zip(me, (dx, dy, dz)))

    def code(rows, slots):
        anchor = decode(encode(rows[:, :, :1]))
        lane = lax.broadcasted_iota(jnp.int32, rows.shape, 2)
        coded = encode(jnp.where(lane == 0, rows, rows - anchor))
        for s in range(2):
            tiles = [coded[:, 4 * s : 4 * s + 4, TILE * j : TILE * (j + 1)] for j in range(4)]
            message = jnp.concatenate(tiles, axis=1).astype(jnp.bfloat16)
            for n, slot in enumerate(slots):
                codes[slot, s] = message[n]

    def place(at):
        return (at[0] * 4 + at[1]) * 4 + at[2]

    def code_some(chips):
        code(jnp.stack([acc[at] for at in chips]), [place(at) for at in chips])

    def emit(at):
        for s in range(2):
            deliver(place(at), s, at)

    def close(k):
        return lax.rem(k + 3, 4)

    for copy in heads:
        copy.wait()
    onward(0)
    multiply(0, 0)
    onward(-1)
    multiply(1, 0)
    onward(1)
    multiply(2, 0)
    onward(2)
    multiply(0, -1, 1)
    last(0)
    multiply(1, -1, 1)
    last(-1)
    multiply(2, -1, 1)
    last(1)

    def near(k, _):
        for dx in (3, 0, 1):
            code_some([chip(dx, close(k), dz) for dz in (3, 0, 1)])
        for dx in (3, 0, 1):
            for dz in (3, 0, 1):
                if (dx, dz) != (0, 0):
                    emit(chip(dx, close(k), dz))
        return 0

    lax.fori_loop(0, 3, near, 0)
    emit(chip(0, 3, 0))
    emit(chip(0, 1, 0))
    own = place(me)
    deliver(own, 1 - core, me)
    got[here] = codes[own, core]

    last(2)
    for part in range(3):
        multiply(part, 2)

    def far(k, _):
        code_some([chip(2, dy, k) for dy in range(4)])
        for dy in range(4):
            emit(chip(2, dy, k))
        return 0

    def rest(k, _):
        code_some([chip(close(k), 2, dz) for dz in range(4)] + [chip(close(k), dy, 2) for dy in (3, 0, 1)])
        for dz in range(4):
            emit(chip(close(k), 2, dz))
        for dy in (3, 0, 1):
            emit(chip(close(k), dy, 2))
        return 0

    lax.fori_loop(0, 3, rest, 0)
    lax.fori_loop(0, 4, far, 0)
    for copy in sent.values():
        copy.wait_send()
    pltpu.make_async_remote_copy(
        got.at[pl.ds(0, 127)], got.at[pl.ds(0, 127)], spread.at[0], spread.at[1],
        device_id=sibling, device_id_type=MESH,
    ).wait()

    def four(rows):
        return jnp.concatenate([rows] * 4, axis=rows.ndim - 2)

    some = 16
    first = lax.broadcasted_iota(jnp.int32, (some, 16, TILE), 2) == 0
    first = first & (lax.broadcasted_iota(jnp.int32, (some, 16, TILE), 1) < 4)

    def open_messages(n, top):
        at = pl.ds(n * some, some)
        d = decode(got[at].astype(jnp.float32))
        values = jnp.where(first, d, d + four(d[:, :4, :1]))
        logits[at] = values
        return jnp.maximum(top, jnp.max(values, axis=0))

    def by_token(rows, combine, reduce):
        each = reduce(rows, axis=1, keepdims=True)
        return combine(combine(each[:4], each[4:8]), combine(each[8:12], each[12:]))

    top = lax.fori_loop(0, 128 // some, open_messages, jnp.full((16, TILE), -jnp.inf, jnp.float32))
    top = by_token(top, jnp.maximum, jnp.max)
    top_rows = jnp.broadcast_to(four(top), (16, TILE))

    def add(n, total):
        return total + jnp.sum(jnp.exp(logits[pl.ds(n * some, some)] - top_rows), axis=0)

    total = lax.fori_loop(0, 128 // some, add, jnp.zeros((16, TILE), jnp.float32))
    total = by_token(total, jnp.add, jnp.sum)
    top_row = jnp.broadcast_to(top, (TOK, TILE))
    log_row = jnp.broadcast_to(jnp.log(total), (TOK, TILE))

    def finish(n, _):
        at = pl.ds(n * some, some)
        for j in range(4):
            out_ref[at, :, TILE * j : TILE * (j + 1)] = logits[at, 4 * j : 4 * j + 4] - top_row - log_row
        return 0

    lax.fori_loop(0, 128 // some, finish, 0)


def on_device(hidden, gain, head):
    log_probs = pl.pallas_call(
        kernel,
        out_shape=jax.ShapeDtypeStruct((128, TOK, V), jnp.float32),
        in_specs=[
            pl.BlockSpec(memory_space=pltpu.VMEM),
            pl.BlockSpec(memory_space=pltpu.VMEM),
            pl.BlockSpec(memory_space=pl.ANY),
        ],
        out_specs=pl.BlockSpec(memory_space=pltpu.VMEM),
        scratch_shapes=[
            pltpu.VMEM((2, 16, D // 8), jnp.bfloat16),
            pltpu.VMEM((2, 16, D // 8), jnp.bfloat16),
            pltpu.VMEM((4, 4, 4, 2, 16, QUARTER), jnp.bfloat16),
            pltpu.VMEM((4, QUARTER, V), jnp.bfloat16),
            pltpu.VMEM((4, 4, 4, 8, V), jnp.float32),
            pltpu.VMEM((64, 2, 16, TILE), jnp.bfloat16),
            pltpu.VMEM((128, 16, TILE), jnp.bfloat16),
            pltpu.VMEM((128, 16, TILE), jnp.float32),
            pltpu.SemaphoreType.DMA((EVENTS,)),
            pltpu.SemaphoreType.DMA((EVENTS,)),
            pltpu.SemaphoreType.DMA((4,)),
            pltpu.SemaphoreType.DMA((2,)),
        ],
        compiler_params=pltpu.CompilerParams(
            collective_id=0, has_side_effects=True, vmem_limit_bytes=50 * 2**20
        ),
        cost_estimate=pl.CostEstimate(
            flops=2 * 512 * D * V, bytes_accessed=D * V * 2, transcendentals=0
        ),
    )(hidden, gain.reshape(1, D), head)
    return log_probs.transpose(1, 0, 2).reshape(TOK, 128 * V)


def solution(mesh):
    return jax.shard_map(
        on_device,
        mesh=mesh,
        in_specs=(P(("grp", "tp"), None), P(), P(None, ("grp", "tp"))),
        out_specs=P(("grp", "tp"), None),
        check_vma=False,
    )
```

time: 180 us -> 65.4 us (0.36)
  waiting for transfers between devices: 92.8 us -> 0 us
  Pallas kernels: 0 us -> 62.6 us
  blocking collectives: 50.8 us -> 0 us
  matrix products: 16.4 us -> 0 us
  between operations: 13.4 us -> 0.01 us
  other arithmetic: 4.83 us -> 0 us
    all_gather x1 -> x0, waiting for transfers between devices: 92.8 us -> none  [on_device(): lax.all_gather(group_block, 'grp', axis=0, tiled=True)]
    pallas_call x0 -> x1, Pallas kernels: none -> 62.6 us  [on_device(): pl.pallas_call(kernel, out_shape=jax.ShapeDtypeStruct((128, TOK, V), jnp....]
    all_to_all x2 -> x0, blocking collectives: 50.8 us -> none  [the longest x1 28.3 us: on_device(): lax.all_to_all(logits, ('grp', 'tp'), split_axis=0, concat_axis=1, tiled=...]
    dot_general x1 -> x0, matrix products: 16.4 us -> none  [on_device(): jnp.dot(lax.all_gather(group_block, 'grp', axis=0, tiled=True), head, pre...]
    unnamed x0 -> x5, local copies, waits for them, and re-layouts: none -> 2.72 us
    reduce_sum x2 -> x0, other arithmetic: 1.89 us -> none  [the longest x1 1.15 us: on_device(): mean_square = jnp.mean(values * values, axis=-1, keepdims=True)]
  transfers between devices with their start and end apart: 1 -> 0, of which waited for: 1 -> 0; matrix products, arithmetic and copies ran while one was open for 0% -> 0% of each run, Pallas kernels for 0% -> 0%
where the time goes in v3:
time: 65.4 us; the launch traced here: 65.3 us
  Pallas kernels  62.6 us (96%)
  local copies, waits for them, and re-layouts  2.72 us (4%)
    pallas_call x1, Pallas kernels, on_device(): pl.pallas_call(kernel, out_shape=jax.ShapeDtypeStruct((128, TOK, V), jnp....  62.6 us
    unnamed x5, local copies, waits for them, and re-layouts  2.72 us

profile of v3, /device:TPU:1, one launch (start us, length us, event | category | flops | bytes accessed | tf_op | source)
XLA Modules:
  0.0 65.3 jit_solution(2396715010984151861)
XLA Ops:
  0.0 0.0 copy-start
  0.0 0.9 %copy-done = bf16[4,16384]{1,0:T(4,128)(2,1)S(1)} copy-done((bf16[4,16384]{1,0:T(4,128)(2,1)S(1)}, bf16[4,16384]{1,0:T(4,128)(2,1)}, u32[]{:S(2)}) %copy-start) | copy-done | bytes 131096
  0.9 0.0 copy-start.1
  0.9 0.8 %copy-done.1 = f32[16384]{0:T(1024)S(1)} copy-done((f32[16384]{0:T(1024)S(1)}, f32[16384]{0:T(1024)}, u32[]{:S(2)}) %copy-start.1) | copy-done | bytes 65560
  1.7 62.6 %shard_map.37 = f32[128,4,512]{2,1,0:T(4,128)S(1)} custom-call(bf16[4,16384]{1,0:T(4,128)(2,1)S(1)} %copy-done, f32[1,16384]{1,0:T(1,128)S(1)} %bitcast.5, bf16[16384,512]{1,0:T(8,128)(2,1)} %head_ref.1), custom_call_target="tpu_custom_call" | custom-call | flops 8589934592 | bytes 16777216 | tf_op jit(solution)/shard_map/pallas_call | solution.py:337
  64.3 1.0 %copy.5 = f32[4,65536]{1,0:T(4,128)} copy(f32[4,65536]{1,0:T(4,128)S(1)} %bitcast.4) | data formatting | bytes 2097152
Async XLA Ops:
  0.0 0.9 %copy-start = (bf16[4,16384]{1,0:T(4,128)(2,1)S(1)}, bf16[4,16384]{1,0:T(4,128)(2,1)}, u32[]{:S(2)}) copy-start(bf16[4,16384]{1,0:T(4,128)(2,1)} %hidden_ref.1) | copy-start | bytes 393220
  0.9 0.8 %copy-start.1 = (f32[16384]{0:T(1024)S(1)}, f32[16384]{0:T(1024)}, u32[]{:S(2)}) copy-start(f32[16384]{0:T(1024)} %param.4) | copy-start | bytes 196612

commit v4 on v3

--- a/solution.py
+++ b/solution.py
@@ -12,7 +12,7 @@
 PARTS = ((0, 11, 6), (11, 22, 17), (22, 32, 27))
 ORDERS = ((0, 1, 2), (1, 2, 0), (2, 0, 1))
 STEEP, FLOOR, LOWEST = 17.5, 8.0, 125.0
-EVENTS = 1 + 3 * 39
+EVENTS = 1 + 3 * 51
 
 
 def position():
@@ -42,10 +42,16 @@
 
 
 def kernel(
-    hidden_ref, gain_ref, head_ref, out_ref, norm, piece, units, head, acc, codes, got, logits, send, recv, local, spread
+    hidden_hbm, gain_hbm, head_ref, out_ref, hidden_ref, gain_ref, norm, piece, units, head, acc, codes, got, logits, send, recv, local, spread
 ):
     me, core = position()
     sibling = device(me, 1 - core)
+    inputs = [
+        pltpu.make_async_copy(hidden_hbm, hidden_ref, local.at[4]),
+        pltpu.make_async_copy(gain_hbm, gain_ref, local.at[5]),
+    ]
+    for copy in inputs:
+        copy.start()
     heads = []
     for quarter in range(4):
         copy = pltpu.make_async_copy(
@@ -60,6 +66,8 @@
     for other in greeted:
         pl.semaphore_signal(barrier, inc=1, device_id=other, device_id_type=MESH)
 
+    for copy in inputs:
+        copy.wait()
     values = hidden_ref[...].astype(jnp.float32)
     scale = lax.rsqrt(jnp.mean(values * values, axis=-1, keepdims=True) + 1e-05)
     wide = D // 8
@@ -134,20 +142,26 @@
     for r in routes:
         for s in (1, -1, 2):
             r.push(("a", s), 0, s, (0, 0, 0))
+    for k, name in ((1, "b"), (2, "c")):
+        for r in routes:
+            for s in (1, -1):
+                r.push((name, 0, s, 0), k, s, (0, 0, 0))
     acc[...] = jnp.zeros_like(acc)
     for r in routes:
         for s in (1, -1, 2):
             r.arrived(("a", s), (-s, 0, 0))
-        for s in (1, -1):
-            r.push(("b", s), 1, s, (None, 0, 0))
+        for da in (1, -1, 2):
+            for s in (1, -1):
+                r.push(("b", 0, s, da), 1, s, (da, 0, 0))
     for r in routes:
         r.share(0, 0)
-    for r in routes:
-        for s in (1, -1):
-            r.push(("c", 0, s), 2, s, (None, 0, 0))
+        for da in (1, -1, 2):
+            for s in (1, -1):
+                r.push(("c", 0, s, da), 2, s, (da, 0, 0))
     for r in routes:
         for s, span in ((1, 0), (-1, 1)):
-            r.arrived(("b", s), (None, -s, 0))
+            for da in (0, 1, -1, 2):
+                r.arrived(("b", 0, s, da), (da, -s, 0))
             r.push(("bb", s), 1, s, (None, -s, 0), span)
     for db in (-1, 1):
         for r in routes:
@@ -164,7 +178,11 @@
     def onward(db):
         for r in routes:
             for s, span in ((1, 0), (-1, 1)):
-                r.arrived(("c", db, s), (None, db, -s))
+                if db == 0:
+                    for da in (0, 1, -1, 2):
+                        r.arrived(("c", db, s, da), (da, db, -s))
+                else:
+                    r.arrived(("c", db, s), (None, db, -s))
                 r.push(("cc", db, s), 2, s, (None, db, -s), span)
             for s in (1, -1):
                 r.share(db, -s)
@@ -204,9 +222,10 @@
     grp, tp = lax.axis_index("grp"), lax.axis_index("tp")
     here = grp * 8 + tp
 
-    def deliver(slot, s, at):
+    def deliver(at, s, arrival):
         pltpu.make_async_remote_copy(
-            codes.at[slot, s], got.at[here], spread.at[0], spread.at[1], device_id=device(at, s), device_id_type=MESH
+            codes.at[place(at), s], got.at[here], spread.at[0], spread.at[arrival],
+            device_id=device(at, s), device_id_type=MESH,
         ).start()
 
     def chip(dx, dy, dz):
@@ -228,9 +247,9 @@
     def code_some(chips):
         code(jnp.stack([acc[at] for at in chips]), [place(at) for at in chips])
 
-    def emit(at):
+    def emit(at, arrival=2):
         for s in range(2):
-            deliver(place(at), s, at)
+            deliver(at, s, arrival)
 
     def close(k):
         return lax.rem(k + 3, 4)
@@ -257,62 +276,92 @@
         for dx in (3, 0, 1):
             for dz in (3, 0, 1):
                 if (dx, dz) != (0, 0):
-                    emit(chip(dx, close(k), dz))
+                    emit(chip(dx, close(k), dz), 1)
         return 0
 
     lax.fori_loop(0, 3, near, 0)
-    emit(chip(0, 3, 0))
-    emit(chip(0, 1, 0))
-    own = place(me)
-    deliver(own, 1 - core, me)
-    got[here] = codes[own, core]
+    emit(chip(0, 3, 0), 1)
+    emit(chip(0, 1, 0), 1)
+    deliver(me, 1 - core, 1)
+    got[here] = codes[place(me), core]
 
     last(2)
-    for part in range(3):
-        multiply(part, 2)
-
-    def far(k, _):
-        code_some([chip(2, dy, k) for dy in range(4)])
-        for dy in range(4):
-            emit(chip(2, dy, k))
+    multiply(0, 2)
+
+    def code_and_emit(*sets):
+        for chips in sets:
+            code_some(chips)
+        for chips in sets:
+            for at in chips:
+                emit(at)
+
+    def z_only(k, _):
+        code_and_emit([chip(close(k), dy, 2) for dy in (3, 0, 1)])
         return 0
 
-    def rest(k, _):
-        code_some([chip(close(k), 2, dz) for dz in range(4)] + [chip(close(k), dy, 2) for dy in (3, 0, 1)])
-        for dz in range(4):
-            emit(chip(close(k), 2, dz))
-        for dy in (3, 0, 1):
-            emit(chip(close(k), dy, 2))
+    lax.fori_loop(0, 3, z_only, 0)
+    multiply(1, 2)
+
+    def x_not_y(k, _):
+        code_and_emit([chip(2, close(k), dz) for dz in (3, 0, 1, 2)])
         return 0
 
-    lax.fori_loop(0, 3, rest, 0)
-    lax.fori_loop(0, 4, far, 0)
-    for copy in sent.values():
-        copy.wait_send()
-    pltpu.make_async_remote_copy(
-        got.at[pl.ds(0, 127)], got.at[pl.ds(0, 127)], spread.at[0], spread.at[1],
-        device_id=sibling, device_id_type=MESH,
-    ).wait()
+    lax.fori_loop(0, 3, x_not_y, 0)
+    multiply(2, 2)
+
+    def y_all(k, _):
+        code_and_emit([chip(2 * k + dx, 2, dz) for dx in (0, 1) for dz in range(4)])
+        return 0
+
+    lax.fori_loop(0, 2, y_all, 0)
+
+    def landed(messages, arrival):
+        some = got.at[pl.ds(0, messages)]
+        return pltpu.make_async_remote_copy(
+            some, some, spread.at[0], spread.at[arrival], device_id=sibling, device_id_type=MESH
+        )
 
     def four(rows):
         return jnp.concatenate([rows] * 4, axis=rows.ndim - 2)
 
     some = 16
-    first = lax.broadcasted_iota(jnp.int32, (some, 16, TILE), 2) == 0
-    first = first & (lax.broadcasted_iota(jnp.int32, (some, 16, TILE), 1) < 4)
-
-    def open_messages(n, top):
-        at = pl.ds(n * some, some)
-        d = decode(got[at].astype(jnp.float32))
+
+    def open_messages(top, chips):
+        slots = []
+        for at in chips:
+            for s in range(2):
+                g, t = device(at, s)
+                slots.append(g * 8 + t)
+        d = decode(jnp.stack([got[slot] for slot in slots]).astype(jnp.float32))
+        first = lax.broadcasted_iota(jnp.int32, d.shape, 2) == 0
+        first = first & (lax.broadcasted_iota(jnp.int32, d.shape, 1) < 4)
         values = jnp.where(first, d, d + four(d[:, :4, :1]))
-        logits[at] = values
+        for n, slot in enumerate(slots):
+            logits[slot] = values[n]
         return jnp.maximum(top, jnp.max(values, axis=0))
+
+    def open_near(k, top):
+        return open_messages(top, [chip(dx, close(k), dz) for dx in (3, 0, 1) for dz in (3, 0, 1)])
+
+    def open_z(k, top):
+        return open_messages(top, [chip(close(k), dy, 2) for dy in (3, 0, 1)])
+
+    def open_x(k, top):
+        return open_messages(top, [chip(2, close(k), dz) for dz in (3, 0, 1, 2)])
+
+    def open_y(k, top):
+        return open_messages(top, [chip(2 * k + dx, 2, dz) for dx in (0, 1) for dz in range(4)])
 
     def by_token(rows, combine, reduce):
         each = reduce(rows, axis=1, keepdims=True)
         return combine(combine(each[:4], each[4:8]), combine(each[8:12], each[12:]))
 
-    top = lax.fori_loop(0, 128 // some, open_messages, jnp.full((16, TILE), -jnp.inf, jnp.float32))
+    landed(53, 1).wait_recv()
+    top = lax.fori_loop(0, 3, open_near, jnp.full((16, TILE), -jnp.inf, jnp.float32))
+    landed(74, 2).wait_recv()
+    top = lax.fori_loop(0, 3, open_z, top)
+    top = lax.fori_loop(0, 3, open_x, top)
+    top = lax.fori_loop(0, 2, open_y, top)
     top = by_token(top, jnp.maximum, jnp.max)
     top_rows = jnp.broadcast_to(four(top), (16, TILE))
 
@@ -331,6 +380,9 @@
         return 0
 
     lax.fori_loop(0, 128 // some, finish, 0)
+    landed(127, 1).wait_send()
+    for copy in sent.values():
+        copy.wait_send()
 
 
 def on_device(hidden, gain, head):
@@ -338,12 +390,14 @@
         kernel,
         out_shape=jax.ShapeDtypeStruct((128, TOK, V), jnp.float32),
         in_specs=[
-            pl.BlockSpec(memory_space=pltpu.VMEM),
-            pl.BlockSpec(memory_space=pltpu.VMEM),
-            pl.BlockSpec(memory_space=pl.ANY),
+            pl.BlockSpec(memory_space=pltpu.HBM),
+            pl.BlockSpec(memory_space=pltpu.HBM),
+            pl.BlockSpec(memory_space=pltpu.HBM),
         ],
         out_specs=pl.BlockSpec(memory_space=pltpu.VMEM),
         scratch_shapes=[
+            pltpu.VMEM((TOK, D), jnp.bfloat16),
+            pltpu.VMEM((1, D), jnp.float32),
             pltpu.VMEM((2, 16, D // 8), jnp.bfloat16),
             pltpu.VMEM((2, 16, D // 8), jnp.bfloat16),
             pltpu.VMEM((4, 4, 4, 2, 16, QUARTER), jnp.bfloat16),
@@ -354,8 +408,8 @@
             pltpu.VMEM((128, 16, TILE), jnp.float32),
             pltpu.SemaphoreType.DMA((EVENTS,)),
             pltpu.SemaphoreType.DMA((EVENTS,)),
-            pltpu.SemaphoreType.DMA((4,)),
-            pltpu.SemaphoreType.DMA((2,)),
+            pltpu.SemaphoreType.DMA((6,)),
+            pltpu.SemaphoreType.DMA((3,)),
         ],
         compiler_params=pltpu.CompilerParams(
             collective_id=0, has_side_effects=True, vmem_limit_bytes=50 * 2**20
@@ -363,7 +417,7 @@
         cost_estimate=pl.CostEstimate(
             flops=2 * 512 * D * V, bytes_accessed=D * V * 2, transcendentals=0
         ),
-    )(hidden, gain.reshape(1, D), head)
+    )(*(pltpu.with_memory_space_constraint(a, pltpu.HBM) for a in (hidden, gain.reshape(1, D), head)))
     return log_probs.transpose(1, 0, 2).reshape(TOK, 128 * V)
 
 

time: 65.4 us -> 62.7 us (0.959)
  local copies, waits for them, and re-layouts: 2.72 us -> 0.97 us
  Pallas kernels: 62.6 us -> 61.6 us
    unnamed x5 -> x1, local copies, waits for them, and re-layouts: 2.72 us -> 0.97 us
    pallas_call x1, Pallas kernels: 62.6 us -> 61.6 us  [on_device(): pl.pallas_call(kernel, out_shape=jax.ShapeDtypeStruct((128, TOK, V), jnp....]
where the time goes in v4:
time: 62.7 us; the launch traced here: 62.6 us
  Pallas kernels  61.6 us (98%)
  local copies, waits for them, and re-layouts  0.97 us (2%)
    pallas_call x1, Pallas kernels, on_device(): pl.pallas_call(kernel, out_shape=jax.ShapeDtypeStruct((128, TOK, V), jnp....  61.6 us

profile of v4, /device:TPU:1, one launch (start us, length us, event | category | flops | bytes accessed | tf_op | source)
XLA Modules:
  0.0 62.6 jit_solution(15692929149859910119)
XLA Ops:
  0.0 61.6 %shard_map.37 = f32[128,4,512]{2,1,0:T(4,128)S(1)} custom-call(bf16[4,16384]{1,0:T(4,128)(2,1)} %hidden_hbm.1, f32[1,16384]{1,0:T(1,128)} %bitcast.5, bf16[16384,512]{1,0:T(8,128)(2,1)} %head_ref.1), custom_call_target="tpu_custom_call" | custom-call | flops 8589934592 | bytes 16777216 | tf_op jit(solution)/shard_map/pallas_call | solution.py:389
  61.6 1.0 %copy.5 = f32[4,65536]{1,0:T(4,128)} copy(f32[4,65536]{1,0:T(4,128)S(1)} %bitcast.4) | data formatting | bytes 2097152

commit v5 on v4

--- a/solution.py
+++ b/solution.py
@@ -184,6 +184,7 @@
                 else:
                     r.arrived(("c", db, s), (None, db, -s))
                 r.push(("cc", db, s), 2, s, (None, db, -s), span)
+        for r in routes:
             for s in (1, -1):
                 r.share(db, -s)
 
@@ -202,22 +203,30 @@
                 r.arrived(("share", db, dc), (None, db, dc), of=1 - core)
         low, high, _ = PARTS[part]
         columns = pl.ds(low * TILE, (high - low) * TILE)
-        for of in (0, 1):
-            for h in (0, 1):
-                rows = []
-                for p in at:
-                    index = [slice(None)] * 3
-                    index[axis] = p
-                    rows.append(units[(*index, of, slice(8 * h, 8 * h + 8), columns)].reshape(128, (high - low) * TILE))
-                product = jnp.dot(
-                    jnp.concatenate(rows, axis=0) if len(rows) > 1 else rows[0],
-                    head[of * 2 + h, columns],
-                    preferred_element_type=jnp.float32,
+        wide = (high - low) * TILE
+        quarters = [(of, h) for of in (0, 1) for h in (0, 1)]
+        rows = []
+        for p in at:
+            index = [slice(None)] * 3
+            index[axis] = p
+            rows.append(
+                jnp.concatenate(
+                    [
+                        units[(*index, of, slice(8 * h, 8 * h + 8), columns)].reshape(128, wide)
+                        for of, h in quarters
+                    ],
+                    axis=1,
                 )
-                for n, p in enumerate(at):
-                    index = [slice(None)] * 3
-                    index[axis] = p
-                    acc[tuple(index)] += product[n * 128 : (n + 1) * 128].reshape(4, 4, 8, V)
+            )
+        product = jnp.dot(
+            jnp.concatenate(rows, axis=0) if len(rows) > 1 else rows[0],
+            jnp.concatenate([head[of * 2 + h, columns] for of, h in quarters], axis=0),
+            preferred_element_type=jnp.float32,
+        )
+        for n, p in enumerate(at):
+            index = [slice(None)] * 3
+            index[axis] = p
+            acc[tuple(index)] += product[n * 128 : (n + 1) * 128].reshape(4, 4, 8, V)
 
     grp, tp = lax.axis_index("grp"), lax.axis_index("tp")
     here = grp * 8 + tp
@@ -326,7 +335,8 @@
 
     some = 16
 
-    def open_messages(top, chips):
+    def open_messages(carry, chips):
+        top, total = carry
         slots = []
         for at in chips:
             for s in range(2):
@@ -338,45 +348,39 @@
         values = jnp.where(first, d, d + four(d[:, :4, :1]))
         for n, slot in enumerate(slots):
             logits[slot] = values[n]
-        return jnp.maximum(top, jnp.max(values, axis=0))
-
-    def open_near(k, top):
-        return open_messages(top, [chip(dx, close(k), dz) for dx in (3, 0, 1) for dz in (3, 0, 1)])
-
-    def open_z(k, top):
-        return open_messages(top, [chip(close(k), dy, 2) for dy in (3, 0, 1)])
-
-    def open_x(k, top):
-        return open_messages(top, [chip(2, close(k), dz) for dz in (3, 0, 1, 2)])
-
-    def open_y(k, top):
-        return open_messages(top, [chip(2 * k + dx, 2, dz) for dx in (0, 1) for dz in range(4)])
+        higher = jnp.maximum(top, jnp.max(values, axis=0))
+        return higher, total * jnp.exp(top - higher) + jnp.sum(jnp.exp(values - higher), axis=0)
+
+    def open_near(k, carry):
+        return open_messages(carry, [chip(dx, close(k), dz) for dx in (3, 0, 1) for dz in (3, 0, 1)])
+
+    def open_z(k, carry):
+        return open_messages(carry, [chip(close(k), dy, 2) for dy in (3, 0, 1)])
+
+    def open_x(k, carry):
+        return open_messages(carry, [chip(2, close(k), dz) for dz in (3, 0, 1, 2)])
+
+    def open_y(k, carry):
+        return open_messages(carry, [chip(2 * k + dx, 2, dz) for dx in (0, 1) for dz in range(4)])
 
     def by_token(rows, combine, reduce):
         each = reduce(rows, axis=1, keepdims=True)
         return combine(combine(each[:4], each[4:8]), combine(each[8:12], each[12:]))
 
+    carry = (jnp.full((16, TILE), -jnp.inf, jnp.float32), jnp.zeros((16, TILE), jnp.float32))
     landed(53, 1).wait_recv()
-    top = lax.fori_loop(0, 3, open_near, jnp.full((16, TILE), -jnp.inf, jnp.float32))
+    carry = lax.fori_loop(0, 3, open_near, carry)
     landed(74, 2).wait_recv()
-    top = lax.fori_loop(0, 3, open_z, top)
-    top = lax.fori_loop(0, 3, open_x, top)
-    top = lax.fori_loop(0, 2, open_y, top)
-    top = by_token(top, jnp.maximum, jnp.max)
-    top_rows = jnp.broadcast_to(four(top), (16, TILE))
-
-    def add(n, total):
-        return total + jnp.sum(jnp.exp(logits[pl.ds(n * some, some)] - top_rows), axis=0)
-
-    total = lax.fori_loop(0, 128 // some, add, jnp.zeros((16, TILE), jnp.float32))
-    total = by_token(total, jnp.add, jnp.sum)
-    top_row = jnp.broadcast_to(top, (TOK, TILE))
-    log_row = jnp.broadcast_to(jnp.log(total), (TOK, TILE))
+    carry = lax.fori_loop(0, 3, open_z, carry)
+    carry = lax.fori_loop(0, 3, open_x, carry)
+    tops, totals = lax.fori_loop(0, 2, open_y, carry)
+    top = jnp.broadcast_to(four(by_token(tops, jnp.maximum, jnp.max)), (16, TILE))
+    total = by_token(totals * jnp.exp(tops - top), jnp.add, jnp.sum)
+    log_total = jnp.broadcast_to(four(jnp.log(total)), (16, TILE))
 
     def finish(n, _):
         at = pl.ds(n * some, some)
-        for j in range(4):
-            out_ref[at, :, TILE * j : TILE * (j + 1)] = logits[at, 4 * j : 4 * j + 4] - top_row - log_row
+        out_ref[at] = logits[at] - top - log_total
         return 0
 
     lax.fori_loop(0, 128 // some, finish, 0)
@@ -388,7 +392,7 @@
 def on_device(hidden, gain, head):
     log_probs = pl.pallas_call(
         kernel,
-        out_shape=jax.ShapeDtypeStruct((128, TOK, V), jnp.float32),
+        out_shape=jax.ShapeDtypeStruct((128, 16, TILE), jnp.float32),
         in_specs=[
             pl.BlockSpec(memory_space=pltpu.HBM),
             pl.BlockSpec(memory_space=pltpu.HBM),
@@ -418,7 +422,7 @@
             flops=2 * 512 * D * V, bytes_accessed=D * V * 2, transcendentals=0
         ),
     )(*(pltpu.with_memory_space_constraint(a, pltpu.HBM) for a in (hidden, gain.reshape(1, D), head)))
-    return log_probs.transpose(1, 0, 2).reshape(TOK, 128 * V)
+    return log_probs.reshape(128 * 4, TOK, TILE).transpose(1, 0, 2).reshape(TOK, 128 * V)
 
 
 def solution(mesh):

time: 62.7 us -> 61.9 us (0.987)
  Pallas kernels: 61.6 us -> 60.8 us
    pallas_call x1, Pallas kernels: 61.6 us -> 60.8 us  [on_device(): pl.pallas_call(kernel, out_shape=jax.ShapeDtypeStruct((128, 16, TILE), jn...]
where the time goes in v5:
time: 61.9 us; the launch traced here: 61.8 us
  Pallas kernels  60.8 us (98%)
  local copies, waits for them, and re-layouts  0.97 us (2%)
    pallas_call x1, Pallas kernels, on_device(): pl.pallas_call(kernel, out_shape=jax.ShapeDtypeStruct((128, 16, TILE), jn...  60.8 us

profile of v5, /device:TPU:1, one launch (start us, length us, event | category | flops | bytes accessed | tf_op | source)
XLA Modules:
  0.0 61.8 jit_solution(14979483594699212835)
XLA Ops:
  0.0 60.8 %shard_map.37 = f32[128,16,128]{2,1,0:T(8,128)S(1)} custom-call(bf16[4,16384]{1,0:T(4,128)(2,1)} %hidden_hbm.1, f32[1,16384]{1,0:T(1,128)} %bitcast.7, bf16[16384,512]{1,0:T(8,128)(2,1)} %head_ref.1), custom_call_target="tpu_custom_call" | custom-call | flops 8589934592 | bytes 16777216 | tf_op jit(solution)/shard_map/pallas_call | solution.py:393
  60.8 1.0 %copy.6 = f32[4,65536]{1,0:T(4,128)} copy(f32[4,65536]{1,0:T(4,128)S(1)} %bitcast.6) | data formatting | bytes 2097152

commit v6 on v5

--- a/solution.py
+++ b/solution.py
@@ -279,18 +279,13 @@
     multiply(2, -1, 1)
     last(1)
 
-    def near(k, _):
-        for dx in (3, 0, 1):
-            code_some([chip(dx, close(k), dz) for dz in (3, 0, 1)])
-        for dx in (3, 0, 1):
-            for dz in (3, 0, 1):
-                if (dx, dz) != (0, 0):
-                    emit(chip(dx, close(k), dz), 1)
-        return 0
-
-    lax.fori_loop(0, 3, near, 0)
-    emit(chip(0, 3, 0), 1)
-    emit(chip(0, 1, 0), 1)
+    near_by = (3, 0, 1)
+    near = [[chip(dx, dy, dz) for dx in near_by for dz in near_by] for dy in near_by]
+    for n, chips in enumerate(near):
+        code_some(chips)
+        for at in chips:
+            if n != 1 or at is not chips[4]:
+                emit(at, 1)
     deliver(me, 1 - core, 1)
     got[here] = codes[place(me), core]
 
@@ -304,25 +299,16 @@
             for at in chips:
                 emit(at)
 
-    def z_only(k, _):
-        code_and_emit([chip(close(k), dy, 2) for dy in (3, 0, 1)])
-        return 0
-
-    lax.fori_loop(0, 3, z_only, 0)
+    z_only = [chip(dx, dy, 2) for dx in near_by for dy in near_by]
+    x_not_y = [chip(2, dy, dz) for dy in near_by for dz in (*near_by, 2)]
+    y_all = [chip(dx, 2, dz) for dx in (2, *near_by) for dz in (2, *near_by)]
+    code_and_emit(z_only)
     multiply(1, 2)
 
-    def x_not_y(k, _):
-        code_and_emit([chip(2, close(k), dz) for dz in (3, 0, 1, 2)])
-        return 0
-
-    lax.fori_loop(0, 3, x_not_y, 0)
+    code_and_emit(x_not_y)
     multiply(2, 2)
 
-    def y_all(k, _):
-        code_and_emit([chip(2 * k + dx, 2, dz) for dx in (0, 1) for dz in range(4)])
-        return 0
-
-    lax.fori_loop(0, 2, y_all, 0)
+    code_and_emit(y_all[:8], y_all[8:])
 
     def landed(messages, arrival):
         some = got.at[pl.ds(0, messages)]
@@ -351,29 +337,18 @@
         higher = jnp.maximum(top, jnp.max(values, axis=0))
         return higher, total * jnp.exp(top - higher) + jnp.sum(jnp.exp(values - higher), axis=0)
 
-    def open_near(k, carry):
-        return open_messages(carry, [chip(dx, close(k), dz) for dx in (3, 0, 1) for dz in (3, 0, 1)])
-
-    def open_z(k, carry):
-        return open_messages(carry, [chip(close(k), dy, 2) for dy in (3, 0, 1)])
-
-    def open_x(k, carry):
-        return open_messages(carry, [chip(2, close(k), dz) for dz in (3, 0, 1, 2)])
-
-    def open_y(k, carry):
-        return open_messages(carry, [chip(2 * k + dx, 2, dz) for dx in (0, 1) for dz in range(4)])
-
     def by_token(rows, combine, reduce):
         each = reduce(rows, axis=1, keepdims=True)
         return combine(combine(each[:4], each[4:8]), combine(each[8:12], each[12:]))
 
     carry = (jnp.full((16, TILE), -jnp.inf, jnp.float32), jnp.zeros((16, TILE), jnp.float32))
     landed(53, 1).wait_recv()
-    carry = lax.fori_loop(0, 3, open_near, carry)
+    for chips in near:
+        carry = open_messages(carry, chips)
     landed(74, 2).wait_recv()
-    carry = lax.fori_loop(0, 3, open_z, carry)
-    carry = lax.fori_loop(0, 3, open_x, carry)
-    tops, totals = lax.fori_loop(0, 2, open_y, carry)
+    for chips in (z_only, x_not_y[:6], x_not_y[6:], y_all[:8], y_all[8:]):
+        carry = open_messages(carry, chips)
+    tops, totals = carry
     top = jnp.broadcast_to(four(by_token(tops, jnp.maximum, jnp.max)), (16, TILE))
     total = by_token(totals * jnp.exp(tops - top), jnp.add, jnp.sum)
     log_total = jnp.broadcast_to(four(jnp.log(total)), (16, TILE))
@@ -383,7 +358,7 @@
         out_ref[at] = logits[at] - top - log_total
         return 0
 
-    lax.fori_loop(0, 128 // some, finish, 0)
+    lax.fori_loop(0, 128 // some, finish, 0, unroll=2)
     landed(127, 1).wait_send()
     for copy in sent.values():
         copy.wait_send()

time: 61.9 us -> 60.6 us (0.979)
  Pallas kernels: 60.8 us -> 59.5 us
    pallas_call x1, Pallas kernels: 60.8 us -> 59.5 us  [on_device(): pl.pallas_call(kernel, out_shape=jax.ShapeDtypeStruct((128, 16, TILE), jn...]
where the time goes in v6:
time: 60.6 us; the launch traced here: 60.5 us
  Pallas kernels  59.5 us (98%)
  local copies, waits for them, and re-layouts  0.97 us (2%)
    pallas_call x1, Pallas kernels, on_device(): pl.pallas_call(kernel, out_shape=jax.ShapeDtypeStruct((128, 16, TILE), jn...  59.5 us

profile of v6, /device:TPU:1, one launch (start us, length us, event | category | flops | bytes accessed | tf_op | source)
XLA Modules:
  0.0 60.5 jit_solution(7166890952738784111)
XLA Ops:
  0.0 59.5 %shard_map.37 = f32[128,16,128]{2,1,0:T(8,128)S(1)} custom-call(bf16[4,16384]{1,0:T(4,128)(2,1)} %hidden_hbm.1, f32[1,16384]{1,0:T(1,128)} %bitcast.7, bf16[16384,512]{1,0:T(8,128)(2,1)} %head_ref.1), custom_call_target="tpu_custom_call" | custom-call | flops 8589934592 | bytes 16777216 | tf_op jit(solution)/shard_map/pallas_call | solution.py:368
  59.5 1.0 %copy.6 = f32[4,65536]{1,0:T(4,128)} copy(f32[4,65536]{1,0:T(4,128)S(1)} %bitcast.6) | data formatting | bytes 2097152

commit v7 on v6

--- a/solution.py
+++ b/solution.py
@@ -175,9 +175,12 @@
             r.push(("c", 2, s), 2, s, (None, 2, 0))
         r.share(2, 0)
 
+    def halves(db):
+        return ((1, 0), (-1, 1)) if db in (0, -1) else ((1, 1), (-1, 0))
+
     def onward(db):
         for r in routes:
-            for s, span in ((1, 0), (-1, 1)):
+            for s, span in halves(db):
                 if db == 0:
                     for da in (0, 1, -1, 2):
                         r.arrived(("c", db, s, da), (da, db, -s))
@@ -190,7 +193,7 @@
 
     def last(db):
         for r in routes:
-            for s, span in ((1, 0), (-1, 1)):
+            for s, span in halves(db):
                 r.arrived(("cc", db, s), (None, db, 2), span)
             r.share(db, 2)
 

time: 60.6 us -> 60.2 us (level)
  no operation moved by 1% of the time
where the time goes in v7:
time: 60.2 us; the launch traced here: 60.1 us
  Pallas kernels  59.1 us (98%)
  local copies, waits for them, and re-layouts  0.97 us (2%)
    pallas_call x1, Pallas kernels, on_device(): pl.pallas_call(kernel, out_shape=jax.ShapeDtypeStruct((128, 16, TILE), jn...  59.1 us

profile of v7, /device:TPU:1, one launch (start us, length us, event | category | flops | bytes accessed | tf_op | source)
XLA Modules:
  0.0 60.1 jit_solution(3594627436027696132)
XLA Ops:
  0.0 59.1 %shard_map.37 = f32[128,16,128]{2,1,0:T(8,128)S(1)} custom-call(bf16[4,16384]{1,0:T(4,128)(2,1)} %hidden_hbm.1, f32[1,16384]{1,0:T(1,128)} %bitcast.7, bf16[16384,512]{1,0:T(8,128)(2,1)} %head_ref.1), custom_call_target="tpu_custom_call" | custom-call | flops 8589934592 | bytes 16777216 | tf_op jit(solution)/shard_map/pallas_call | solution.py:371
  59.1 1.0 %copy.6 = f32[4,65536]{1,0:T(4,128)} copy(f32[4,65536]{1,0:T(4,128)S(1)} %bitcast.6) | data formatting | bytes 2097152
